TPU v7x, 1024 devices: a whole 4x8x16 slice. The times are simulated.
1024 devices in a mesh: dp: 64 (over y_lo, z), expert: 16 (over y_hi, x, core).
Axes of the slice: x: 4, y: 8 (y_hi: 2, y_lo: 4; y = y_hi * 4 + y_lo), z: 16, core: 2. Of those that a mesh axis runs over, the one named last changes fastest.
Arguments:
- d_out: bfloat16 [131072, 4096], P(('dp', 'expert')), may hold values from -6 to 6
- logits: float32 [131072, 16], P(('dp', 'expert')), may hold values from -6 to 6
- routes: int32 [131072, 2], P(('dp', 'expert')), may hold values from 0 to 15, as said below
- slots: int32 [131072, 2], P(('dp', 'expert')), may hold values from 0 to 15, as said below
- state_map: bfloat16 [4096, 16], replicated, may hold values from -0.09375 to 0.09375
- channels: bfloat16 [16384, 8192], P(('dp', 'expert')), may hold values from -0.5 to 0.5
Outputs:
- expert_grads: bfloat16 [64, 16, 16, 16, 4096], P('dp', 'expert')
- mamba_grad: float32 [16, 8192], P(None, 'expert')
Inputs may be any that keep to these rules, and one draw needn't show every extreme that they name: `routes`: on one device a token's two experts differ, every expert is named by exactly 16 of the device's choices, and a token's second expert is a fixed function of its first on each device. On one device the choices of one expert hold the slots 0 to 15, each once.
All inputs are finite; a program needn't handle non-finite values.
Results may differ from a plain program's by a relative error of at most 0.0032.
Values may be sent and summed in bfloat16 or wider, within the bound.
A program may use at most 32 MiB of HBM per device.

v0:
```python
import jax
import jax.numpy as jnp
from jax import lax
from jax.sharding import PartitionSpec as P


def shards(d_out, logits, routes, slots, state_map, channels):
    tokens = d_out.shape[0]
    experts = logits.shape[1]
    capacity = 2 * tokens // experts
    expert_ids = jnp.arange(experts, dtype=jnp.int32)
    selected = jnp.sum(
        jnp.where(
            routes[:, :, None] == expert_ids[None, None, :], logits[:, None, :], jnp.float32(0.0)
        ),
        axis=2,
    )
    weights = jnp.stack(
        [
            jax.nn.sigmoid(selected[:, 0] - selected[:, 1]),
            jax.nn.sigmoid(selected[:, 1] - selected[:, 0]),
        ],
        axis=1,
    )
    pieces = (weights[:, :, None] * d_out[:, None, :].astype(jnp.float32)).astype(jnp.bfloat16)
    target = routes * capacity + slots
    one_hot = (
        target[None, :, :] == jnp.arange(experts * capacity, dtype=jnp.int32)[:, None, None]
    ).astype(jnp.bfloat16)
    buffer = jnp.einsum("rtk,tkd->rd", one_hot, pieces, preferred_element_type=jnp.float32)
    buffer = buffer.astype(jnp.bfloat16).reshape(experts, capacity, d_out.shape[1])
    received = lax.all_to_all(buffer, "expert", split_axis=0, concat_axis=0, tiled=True)
    expert_grads = received[None, None]
    mamba_rows = d_out[: channels.shape[0]]
    state_cot = jnp.dot(mamba_rows, state_map, preferred_element_type=jnp.float32).astype(
        jnp.bfloat16
    )
    partial_value = lax.dot_general(
        state_cot, channels, (((0,), (0,)), ((), ())), preferred_element_type=jnp.float32
    )
    columns = partial_value.shape[1] // lax.axis_size("expert")
    summed = lax.psum(partial_value, ("dp", "expert"))
    gradient = lax.dynamic_slice_in_dim(summed, lax.axis_index("expert") * columns, columns, 1)
    return (expert_grads, gradient)


def solution(mesh):
    return jax.shard_map(
        shards,
        mesh=mesh,
        in_specs=(
            P(("dp", "expert"), None),
            P(("dp", "expert"), None),
            P(("dp", "expert"), None),
            P(("dp", "expert"), None),
            P(),
            P(("dp", "expert"), None),
        ),
        out_specs=(P("dp", "expert", None, None, None), P(None, "expert")),
        check_vma=False,
    )
```

profile of v0, /device:TPU:56, one launch (start us, length us, event | category | flops | bytes accessed | tf_op | source)
XLA Modules:
  0.0 527.8 jit_solution(6918391576699537014)
XLA Ops:
  7.2 0.0 copy-start
  7.2 0.0 copy-start.2
  7.2 0.0 copy-start.3
  7.2 0.0 copy-start.4
  7.2 1.5 convert_element_type.14
  8.7 0.0 copy-done.2
  8.7 0.0 copy-done.3
  8.7 0.0 copy-done.4
  8.8 2.1 fusion
  10.9 0.0 copy-start.1
  10.9 9.8 %all-to-all-start = ((bf16[16,16,4096]{2,1,0:T(8,128)(2,1)}), bf16[16,16,4096]{2,1,0:T(8,128)(2,1)S(1)}, u32[]{:S(2)}, u32[]{:S(2)}) async-start(bf16[16,16,4096]{2,1,0:T(8,128)(2,1)} %bitcast.9), calls=%async_computation | async-start | bytes 4194304 | tf_op jit(solution)/shard_map/all_to_all | solution.py:32
  20.7 0.0 all-reduce.2.cloned.1.call-start
  20.8 0.0 copy-done
  20.8 0.0 copy-done.1
  20.8 2.2 fusion.3
  23.0 0.0 all-reduce.2.cloned.1.call-update
  23.0 495.2 %all-reduce.2.cloned.1.call-done = f32[16,8192]{1,0:T(8,128)} async-done(((f32[16,8192]{1,0:T(8,128)}), f32[16,8192]{1,0:T(8,128)}) %all-reduce.2.cloned.1.call-update) | async-done | bytes 524304 | tf_op jit(solution)/shard_map/psum | solution.py:42
  518.2 1.4 constant_dynamic-slice_fusion
  519.6 0.0 all-to-all-done
  519.6 1.3 copy.12
  (4 shorter events, 0.0 us)
Async XLA Ops:
  7.2 13.6 %copy-start = (bf16[16,8192]{1,0:T(8,128)(2,1)S(1)}, bf16[16,8192]{1,0:T(8,128)(2,1)}, u32[]{:S(2)}) copy-start(bf16[16,8192]{1,0:T(8,128)(2,1)} %param.11) | copy-start | bytes 786436
  7.2 1.5 copy-start.2
  7.2 1.5 copy-start.3
  7.2 1.5 copy-start.4
  10.9 9.9 %copy-start.1 = (bf16[4096,16]{0,1:T(8,128)(2,1)S(1)}, bf16[4096,16]{0,1:T(8,128)(2,1)}, u32[]{:S(2)}) copy-start(bf16[4096,16]{0,1:T(8,128)(2,1)} %param.10) | copy-start | bytes 393220
  10.9 508.7 %all-to-all-start = ((bf16[16,16,4096]{2,1,0:T(8,128)(2,1)}), bf16[16,16,4096]{2,1,0:T(8,128)(2,1)S(1)}, u32[]{:S(2)}, u32[]{:S(2)}) async-start(bf16[16,16,4096]{2,1,0:T(8,128)(2,1)} %bitcast.9), calls=%async_computation | async-start | bytes 4194304 | tf_op jit(solution)/shard_map/all_to_all | solution.py:32
  20.7 497.5 %all-reduce.2.cloned.1.call-start = ((), (), s32[]{:S(2)}) async-start(), calls=%async_computation.1 | async-start | bytes 1048576 | tf_op jit(solution)/shard_map/psum | solution.py:42
Sparse Core Ops, SparseCore 0:
  27.0 491.1 all-reduce.1
where the time goes:
time: 529 us; the launch traced here: 528 us
  waiting for transfers between devices  495 us (94%)
  between operations  14.1 us (3%)
  starting transfers between devices  9.85 us (2%)
    psum x1, waiting for transfers between devices, shards(): summed = lax.psum(partial_value, ('dp', 'expert'))  495 us
  transfers between devices with their start and end apart: 2, of which 1 were waited for; matrix products, arithmetic and copies ran while one was open for 1% of the time, Pallas kernels for 0%

commit v1 on v0

v1 whole, which is shorter than its diff:
```python
import jax
import jax.numpy as jnp
from jax import lax
from jax.experimental import pallas as pl
from jax.experimental.pallas import tpu as pltpu
from jax.sharding import PartitionSpec as P

MESH = pl.DeviceIdType.MESH
NX, NY, NZ, NC = 4, 8, 16, 2
EXPERTS, CAP, D = 16, 16, 4096
ROW = NX * NC
BLOCK = 512
TILE = 512

FAR = [(1, dx, dc) for dx in (2, 1, 3, 0) for dc in (0, 1)]
NEAR = [(0, dx, dc) for dx in (2, 1, 3, 0) for dc in (0, 1) if (dx, dc) != (0, 0)]
BULK = [pair[i] for i in range(8) for pair in (FAR, NEAR) if i < len(pair)]
CUTS = (4, 8, 11)
ALONG_Z = [s * k % NZ for k in range(1, 9) for s in (1, -1) if not (k == 8 and s < 0)]
ALONG_Y = (4, 3, 5, 2, 6, 1, 7)


def kernel(
    d_hbm, logits_hbm, routes_hbm, slots_hbm, map_hbm, channels_hbm,
    out, grad,
    d, logits, routes, slots, state_map, channels, pack,
    rows_out, rows_in, z_out, z_in, y_out, y_in, f_out, f_in,
    load_sem, own_sem, b_send, b_recv, r_send, r_recv, z_send, z_recv, y_send, y_recv, f_send, f_recv,
):
    dp, me = lax.axis_index("dp"), lax.axis_index("expert")
    z, y_lo = lax.rem(dp, NZ), dp // NZ
    y_hi, row = me // ROW, lax.rem(me, ROW)
    x, c = row // NC, lax.rem(row, NC)
    y = y_hi * 4 + y_lo

    def peer(dy, dx, dc):
        return (
            lax.rem(y_hi + dy, 2) * ROW + lax.rem(x + dx, NX) * NC + lax.rem(c + dc, NC)
        )

    def at_z(other):
        return (y_lo * NZ + other, me)

    def at_y(other):
        return (lax.rem(other, 4) * NZ + z, (other // 4) * ROW + row)

    barrier = pltpu.get_barrier_semaphore()

    def greet(device):
        pl.semaphore_signal(barrier, inc=1, device_id=device, device_id_type=MESH)

    greeted = 0
    for offsets in BULK:
        greet((dp, peer(*offsets)))
        greeted += 1
    for k in ALONG_Z:
        greet(at_z(lax.rem(z + k, NZ)))
        greeted += 1
    for k in ALONG_Y:
        if k != 4:
            greet(at_y(lax.rem(y + k, NY)))
            greeted += 1

    loads = [
        pltpu.make_async_copy(source, target, load_sem.at[i])
        for i, (source, target) in enumerate(
            [
                (logits_hbm, logits),
                (routes_hbm, routes),
                (slots_hbm, slots),
                (d_hbm, d),
                (channels_hbm, channels),
                (map_hbm, state_map),
            ]
        )
    ]
    for load in loads:
        load.start()
    for load in loads[:3]:
        load.wait()

    expert_ids = lax.broadcasted_iota(jnp.int32, (EXPERTS, 128), 0)
    picked = [
        jnp.sum(
            jnp.where(expert_ids == routes[k : k + 1, :], logits[...], 0.0),
            axis=0,
            keepdims=True,
        )
        for k in range(2)
    ]
    weights = [
        jax.nn.sigmoid(picked[0] - picked[1]),
        jax.nn.sigmoid(picked[1] - picked[0]),
    ]
    target = [routes[k : k + 1, :] * CAP + slots[k : k + 1, :] for k in range(2)]

    def route(half):
        ids = lax.broadcasted_iota(jnp.int32, (128, 128), 0) + half * 128
        hit = [ids == target[k] for k in range(2)]
        chosen = jnp.where(hit[0] | hit[1], 1.0, 0.0).astype(jnp.bfloat16)
        scale = jnp.where(hit[0], weights[0], 0.0) + jnp.where(hit[1], weights[1], 0.0)
        return chosen, jnp.sum(scale, axis=1, keepdims=True)

    def pack_half(half):
        chosen, scale = route(half)
        for i in range(D // TILE):
            columns = slice(i * TILE, (i + 1) * TILE)
            rows = jnp.dot(chosen, d[:, columns], preferred_element_type=jnp.float32)
            pack[pl.ds(half * 8, 8), :, columns] = (
                (rows * scale).astype(jnp.bfloat16).reshape(8, CAP, TILE)
            )

    loads[3].wait()
    pack_half(1 - y_hi)

    loads[4].wait()
    loads[5].wait()
    state_cot = lax.dot_general(
        d[0:16, :], state_map[...], (((1,), (1,)), ((), ())),
        preferred_element_type=jnp.float32,
    ).astype(jnp.bfloat16)
    spread = (
        lax.broadcasted_iota(jnp.int32, (16, 128), 0)
        == lax.broadcasted_iota(jnp.int32, (16, 128), 1)
    ).astype(jnp.bfloat16)
    wide = jnp.dot(state_cot, spread, preferred_element_type=jnp.float32).astype(
        jnp.bfloat16
    )
    for i in range(ROW):
        for b in range(2):
            begin = (b * ROW + i) * BLOCK
            rows_out[i, :, b * BLOCK : (b + 1) * BLOCK] = channels[:, begin : begin + BLOCK]
        rows_out[i, :, 2 * BLOCK :] = wide

    pl.semaphore_wait(barrier, greeted)

    def send(source, destination, send_sem, recv_sem, device):
        copy = pltpu.make_async_remote_copy(
            src_ref=source,
            dst_ref=destination,
            send_sem=send_sem,
            recv_sem=recv_sem,
            device_id=device,
            device_id_type=MESH,
        )
        return copy

    def bulk(offsets):
        other = peer(*offsets)
        return send(pack.at[other], out.at[me], b_send.at[other], b_recv.at[me], (dp, other))

    def bulk_in(offsets):
        other = peer(*offsets)
        return send(pack.at[other], out.at[other], b_send.at[other], b_recv.at[other], (dp, other))

    for offsets in FAR[:1]:
        bulk(offsets).start()
    for _, dx, dc in NEAR:
        other = lax.rem(x + dx, NX) * NC + lax.rem(c + dc, NC)
        send(
            rows_out.at[other], rows_in.at[row], r_send.at[other], r_recv.at[row],
            (dp, y_hi * ROW + other),
        ).start()
    rows_in[row] = rows_out[row]
    pack_half(y_hi)
    own = pltpu.make_async_copy(pack.at[me], out.at[me], own_sem)
    own.start()
    for offsets in BULK[1 : CUTS[0]]:
        bulk(offsets).start()

    for _, dx, dc in NEAR:
        other = lax.rem(x + dx, NX) * NC + lax.rem(c + dc, NC)
        copy = send(
            rows_out.at[other], rows_in.at[other], r_send.at[other], r_recv.at[other],
            (dp, y_hi * ROW + other),
        )
        copy.wait_recv()
    cot = rows_in[:, :, 2 * BLOCK :].reshape(ROW * 16, 128)
    cot = cot.astype(jnp.float32).T[0:16, :].astype(jnp.bfloat16)
    partial = jnp.dot(
        cot, rows_in[:, :, : 2 * BLOCK].reshape(ROW * 16, 2 * BLOCK),
        preferred_element_type=jnp.float32,
    )
    for h in range(2):
        for q in range(8):
            z_out[h * 8 + q] = partial[h * 8 : (h + 1) * 8, q * 128 : (q + 1) * 128]
    for k in ALONG_Z:
        other = lax.rem(z + k, NZ)
        send(z_out.at[other], z_in.at[z], z_send.at[other], z_recv.at[z], at_z(other)).start()
    for offsets in BULK[CUTS[0] : CUTS[1]]:
        bulk(offsets).start()
    z_in[z] = z_out[z]

    for k in ALONG_Z:
        other = lax.rem(z + k, NZ)
        send(z_out.at[other], z_in.at[other], z_send.at[other], z_recv.at[other], at_z(other)).wait_recv()
    total = jnp.sum(z_in[...], axis=0)
    y_out[...] = total
    half = lax.rem(z, 8) // 4
    for k in ALONG_Y:
        other = lax.rem(y + k, NY)

        @pl.when(other // 4 == half)
        def _():
            send(y_out, y_in.at[y], y_send.at[other], y_recv.at[y], at_y(other)).start()

    for offsets in BULK[CUTS[1] : CUTS[2]]:
        bulk(offsets).start()
    y_in[y] = total

    @pl.when(y_hi == half)
    def _():
        for k in ALONG_Y:
            other = lax.rem(y + k, NY)
            send(y_out, y_in.at[other], y_send.at[other], y_recv.at[other], at_y(other)).wait_recv()
        summed = jnp.sum(y_in[...], axis=0)
        f_out[...] = summed
        for k in ALONG_Z:
            other = lax.rem(z + k, NZ)
            send(f_out, f_in.at[z], f_send.at[other], f_recv.at[z], at_z(other)).start()
        f_in[z] = summed

    for offsets in BULK[CUTS[2] :]:
        bulk(offsets).start()

    for h in range(2):
        for q in range(4):
            other = h * 8 + y_hi * 4 + q

            @pl.when(other != z)
            def _():
                send(f_out, f_in.at[other], f_send.at[other], f_recv.at[other], at_z(other)).wait_recv()

    for h in range(2):
        for q in range(4):
            grad[h * 8 : (h + 1) * 8, q * 128 : (q + 1) * 128] = f_in[h * 8 + y_hi * 4 + q]

    for _, dx, dc in NEAR:
        other = lax.rem(x + dx, NX) * NC + lax.rem(c + dc, NC)
        send(
            rows_out.at[other], rows_in.at[row], r_send.at[other], r_recv.at[row],
            (dp, y_hi * ROW + other),
        ).wait_send()
    for k in ALONG_Z:
        other = lax.rem(z + k, NZ)
        send(z_out.at[other], z_in.at[z], z_send.at[other], z_recv.at[z], at_z(other)).wait_send()
    for k in ALONG_Y:
        other = lax.rem(y + k, NY)

        @pl.when(other // 4 == half)
        def _():
            send(y_out, y_in.at[y], y_send.at[other], y_recv.at[y], at_y(other)).wait_send()

    @pl.when(y_hi == half)
    def _():
        for k in ALONG_Z:
            other = lax.rem(z + k, NZ)
            send(f_out, f_in.at[z], f_send.at[other], f_recv.at[z], at_z(other)).wait_send()

    own.wait()
    for offsets in BULK:
        bulk(offsets).wait_send()
        bulk_in(offsets).wait_recv()


def shards(d_out, logits, routes, slots, state_map, channels):
    anywhere = pl.BlockSpec(memory_space=pl.ANY)
    in_hbm = pl.BlockSpec(memory_space=pltpu.HBM)
    bf16, f32 = jnp.bfloat16, jnp.float32
    dma = pltpu.SemaphoreType.DMA
    received, grad = pl.pallas_call(
        kernel,
        out_shape=(
            jax.ShapeDtypeStruct((EXPERTS, CAP, D), bf16),
            jax.ShapeDtypeStruct((16, BLOCK), f32),
        ),
        in_specs=[in_hbm] * 6,
        out_specs=(anywhere, pl.BlockSpec(memory_space=pltpu.VMEM)),
        scratch_shapes=[
            pltpu.VMEM((128, D), bf16),
            pltpu.VMEM((EXPERTS, 128), f32),
            pltpu.VMEM((2, 128), jnp.int32),
            pltpu.VMEM((2, 128), jnp.int32),
            pltpu.VMEM((16, D), bf16),
            pltpu.VMEM((16, EXPERTS * BLOCK), bf16),
            pltpu.VMEM((EXPERTS, CAP, D), bf16),
            pltpu.VMEM((ROW, 16, 2 * BLOCK + 128), bf16),
            pltpu.VMEM((ROW, 16, 2 * BLOCK + 128), bf16),
            pltpu.VMEM((NZ, 8, 128), f32),
            pltpu.VMEM((NZ, 8, 128), f32),
            pltpu.VMEM((8, 128), f32),
            pltpu.VMEM((NY, 8, 128), f32),
            pltpu.VMEM((8, 128), f32),
            pltpu.VMEM((NZ, 8, 128), f32),
            dma((6,)), dma,
            dma((EXPERTS,)), dma((EXPERTS,)),
            dma((ROW,)), dma((ROW,)),
            dma((NZ,)), dma((NZ,)),
            dma((NY,)), dma((NY,)),
            dma((NZ,)), dma((NZ,)),
        ],
        compiler_params=pltpu.CompilerParams(
            collective_id=0, has_side_effects=True, vmem_limit_bytes=24 << 20
        ),
        cost_estimate=pl.CostEstimate(
            flops=300_000_000, bytes_accessed=8_000_000, transcendentals=256
        ),
    )(d_out, logits.T, routes.T, slots.T, state_map.T, channels)
    return received[None, None], grad


def solution(mesh):
    return jax.shard_map(
        shards,
        mesh=mesh,
        in_specs=(
            P(("dp", "expert"), None),
            P(("dp", "expert"), None),
            P(("dp", "expert"), None),
            P(("dp", "expert"), None),
            P(),
            P(("dp", "expert"), None),
        ),
        out_specs=(P("dp", "expert", None, None, None), P(None, "expert")),
        check_vma=False,
    )
```

time: 529 us -> 92.4 us (0.17)
  the two profiles are of different devices: /device:TPU:56 before, /device:TPU:52 now
where the time goes in v1:
time: 92.4 us; the launch traced here: 92.1 us
  Pallas kernels  84.4 us (91%)
  local copies, waits for them, and re-layouts  7.06 us (8%)
    pallas_call x1, Pallas kernels, shards(): pl.pallas_call(kernel, out_shape=(jax.ShapeDtypeStruct((EXPERTS, CAP, D),...  84.4 us
    unnamed x14, local copies, waits for them, and re-layouts  7.06 us

profile of v1, /device:TPU:52, one launch (start us, length us, event | category | flops | bytes accessed | tf_op | source)
XLA Modules:
  0.0 92.1 jit_solution(4284932200967359809)
XLA Ops:
  0.6 0.0 copy-start
  0.6 1.2 %copy-done = bf16[128,4096]{1,0:T(8,128)(2,1)S(1)} copy-done((bf16[128,4096]{1,0:T(8,128)(2,1)S(1)}, bf16[128,4096]{1,0:T(8,128)(2,1)}, u32[]{:S(2)}) %copy-start) | copy-done | bytes 1048600
  1.9 0.0 copy-start.1
  1.9 0.9 %copy-done.1 = bf16[16,8192]{1,0:T(8,128)(2,1)S(1)} copy-done((bf16[16,8192]{1,0:T(8,128)(2,1)S(1)}, bf16[16,8192]{1,0:T(8,128)(2,1)}, u32[]{:S(2)}) %copy-start.1) | copy-done | bytes 262168
  2.8 0.0 copy-start.2
  2.8 0.9 copy-done.2
  3.7 0.0 copy-start.3
  3.7 0.7 copy-done.3
  4.4 0.0 copy-start.4
  4.4 0.7 copy-done.4
  5.1 0.0 copy-start.5
  5.1 0.7 copy-done.5
  5.8 84.4 %shard_map.77 = (bf16[16,16,4096]{2,1,0:T(8,128)(2,1)S(1)}, f32[16,512]{1,0:T(8,128)S(1)}) custom-call(bf16[128,4096]{1,0:T(8,128)(2,1)S(1)} %copy-done, f32[16,128]{1,0:T(8,128)S(1)} %bitcast.7, s32[2,128]{1,0:T(2,128)S(1)} %bitcast.8, s32[2,128]{1,0:T(2,128)S(1)} %bitcast.9, bf16[16,4096]{1,0:T(8,128)(2,1)S(1)} %bitcast.6, bf16[16,8192]{1,0:T(8,128)(2,1)S(1)} %copy-done.1), custom_call_target="tpu_custom_call" | custom-call | flops 300000000 | bytes 8000000 | tf_op jit(solution)/shard_map/pallas_call | solution.py:271
  90.2 1.3 %copy.10 = bf16[1,1,16,16,4096]{4,3,2,1,0:T(8,128)(2,1)} copy(bf16[1,1,16,16,4096]{4,3,2,1,0:T(8,128)(2,1)S(1)} %bitcast.5) | data formatting | bytes 4194304
  91.5 0.6 copy.11
Async XLA Ops:
  0.6 1.2 %copy-start = (bf16[128,4096]{1,0:T(8,128)(2,1)S(1)}, bf16[128,4096]{1,0:T(8,128)(2,1)}, u32[]{:S(2)}) copy-start(bf16[128,4096]{1,0:T(8,128)(2,1)} %d_hbm.1) | copy-start | bytes 3145732
  1.9 0.9 %copy-start.1 = (bf16[16,8192]{1,0:T(8,128)(2,1)S(1)}, bf16[16,8192]{1,0:T(8,128)(2,1)}, u32[]{:S(2)}) copy-start(bf16[16,8192]{1,0:T(8,128)(2,1)} %channels_hbm.1) | copy-start | bytes 786436
  2.8 0.9 copy-start.2
  3.7 0.7 copy-start.3
  4.4 0.7 copy-start.4
  5.1 0.7 copy-start.5

commit v2 on v1

--- a/solution.py
+++ b/solution.py
@@ -14,9 +14,16 @@
 
 FAR = [(1, dx, dc) for dx in (2, 1, 3, 0) for dc in (0, 1)]
 NEAR = [(0, dx, dc) for dx in (2, 1, 3, 0) for dc in (0, 1) if (dx, dc) != (0, 0)]
-BULK = [pair[i] for i in range(8) for pair in (FAR, NEAR) if i < len(pair)]
-CUTS = (4, 8, 11)
+PEERS = FAR + NEAR
+PARTS = 2
+MIX = [pair[i] for i in range(8) for pair in (FAR, NEAR) if i < len(pair)]
+BULK = [(*offsets, q) for q in range(PARTS) for offsets in MIX]
+FIRST = 1
+EXTRA = ((14, 14, 4),)
+CUTS = (14, 26, 30)
+DO_M = True
 ALONG_Z = [s * k % NZ for k in range(1, 9) for s in (1, -1) if not (k == 8 and s < 0)]
+ROLES = 4
 ALONG_Y = (4, 3, 5, 2, 6, 1, 7)
 
 
@@ -25,7 +32,7 @@
     out, grad,
     d, logits, routes, slots, state_map, channels, pack,
     rows_out, rows_in, z_out, z_in, y_out, y_in, f_out, f_in,
-    load_sem, own_sem, b_send, b_recv, r_send, r_recv, z_send, z_recv, y_send, y_recv, f_send, f_recv,
+    load_sem, own_sem, later, first, line, b_send, b_recv, r_send, r_recv, z_send, z_recv, y_send, y_recv, f_send, f_recv,
 ):
     dp, me = lax.axis_index("dp"), lax.axis_index("expert")
     z, y_lo = lax.rem(dp, NZ), dp // NZ
@@ -33,7 +40,7 @@
     x, c = row // NC, lax.rem(row, NC)
     y = y_hi * 4 + y_lo
 
-    def peer(dy, dx, dc):
+    def peer(dy, dx, dc, part=0):
         return (
             lax.rem(y_hi + dy, 2) * ROW + lax.rem(x + dx, NX) * NC + lax.rem(c + dc, NC)
         )
@@ -49,17 +56,29 @@
     def greet(device):
         pl.semaphore_signal(barrier, inc=1, device_id=device, device_id_type=MESH)
 
-    greeted = 0
-    for offsets in BULK:
-        greet((dp, peer(*offsets)))
-        greeted += 1
-    for k in ALONG_Z:
-        greet(at_z(lax.rem(z + k, NZ)))
-        greeted += 1
+    corner = (row == 0) & (y == 0)
+    rank = jnp.where(corner, lax.rem(z + NZ - 1, NZ), z)
+
+    for offsets in PEERS:
+
+        @pl.when(me != 0)
+        def _():
+            greet((dp, peer(*offsets)))
+
     for k in ALONG_Y:
         if k != 4:
-            greet(at_y(lax.rem(y + k, NY)))
-            greeted += 1
+
+            @pl.when(y != 0)
+            def _():
+                greet(at_y(lax.rem(y + k, NY)))
+
+    for k in range(1, NZ):
+
+        @pl.when(rank + k < NZ)
+        def _():
+            greet(at_z(lax.rem(z + k, NZ)))
+
+    greeted = rank + jnp.where(me == 0, 15, 14) + jnp.where((y == 0) | (y == 4), 6, 5)
 
     loads = [
         pltpu.make_async_copy(source, target, load_sem.at[i])
@@ -134,6 +153,28 @@
 
     pl.semaphore_wait(barrier, greeted)
 
+    def tell(semaphore, device):
+        pl.semaphore_signal(semaphore, inc=1, device_id=device, device_id_type=MESH)
+
+    for offsets in PEERS:
+
+        @pl.when(me == 0)
+        def _():
+            tell(first, (dp, peer(*offsets)))
+
+    for k in ALONG_Y:
+        if k != 4:
+
+            @pl.when(y == 0)
+            def _():
+                tell(line, at_y(lax.rem(y + k, NY)))
+
+    for k in range(1, NZ):
+
+        @pl.when(k <= rank)
+        def _():
+            tell(later, at_z(lax.rem(z + NZ - k, NZ)))
+
     def send(source, destination, send_sem, recv_sem, device):
         copy = pltpu.make_async_remote_copy(
             src_ref=source,
@@ -145,28 +186,73 @@
         )
         return copy
 
+    def block(offsets, at):
+        return to(peer(*offsets), offsets[3], at)
+
+    def to(other, q, at):
+        columns = pl.ds(q * (D // PARTS), D // PARTS)
+        return send(
+            pack.at[other, :, columns], out.at[at(other), :, columns],
+            b_send.at[other, q], b_recv.at[at(other), q], (dp, other),
+        )
+
+    def to_first(q):
+        return to(0, q, lambda other: me)
+
     def bulk(offsets):
-        other = peer(*offsets)
-        return send(pack.at[other], out.at[me], b_send.at[other], b_recv.at[me], (dp, other))
+        return block(offsets, lambda other: me)
 
     def bulk_in(offsets):
-        other = peer(*offsets)
-        return send(pack.at[other], out.at[other], b_send.at[other], b_recv.at[other], (dp, other))
-
-    for offsets in FAR[:1]:
-        bulk(offsets).start()
+        return block(offsets, lambda other: other)
+
+    def start(parts):
+        for offsets in parts:
+
+            @pl.when(peer(*offsets) != 0)
+            def _():
+                bulk(offsets).start()
+
+    start(BULK[:FIRST])
+    def across(other):
+        return send(
+            rows_out.at[other], rows_in.at[row], r_send.at[other], r_recv.at[row],
+            (dp, y_hi * ROW + other),
+        )
+
     for _, dx, dc in NEAR:
         other = lax.rem(x + dx, NX) * NC + lax.rem(c + dc, NC)
-        send(
-            rows_out.at[other], rows_in.at[row], r_send.at[other], r_recv.at[row],
-            (dp, y_hi * ROW + other),
-        ).start()
+
+        @pl.when(y_hi * ROW + other != 0)
+        def _():
+            across(other).start()
+
     rows_in[row] = rows_out[row]
     pack_half(y_hi)
     own = pltpu.make_async_copy(pack.at[me], out.at[me], own_sem)
     own.start()
-    for offsets in BULK[1 : CUTS[0]]:
-        bulk(offsets).start()
+    start(BULK[FIRST : CUTS[0]])
+
+    def extra(i, early):
+        begin, end, below = EXTRA[i]
+
+        @pl.when((z < below) == early)
+        def _():
+            start(BULK[begin:end])
+
+    for i in range(len(EXTRA)):
+        extra(i, True)
+
+    @pl.when(me != 0)
+    def _():
+        pl.semaphore_wait(first, 1)
+
+        @pl.when(y_hi == 0)
+        def _():
+            across(0).start()
+
+        for q in range(PARTS):
+            to_first(q).start()
+
 
     for _, dx, dc in NEAR:
         other = lax.rem(x + dx, NX) * NC + lax.rem(c + dc, NC)
@@ -181,34 +267,63 @@
         cot, rows_in[:, :, : 2 * BLOCK].reshape(ROW * 16, 2 * BLOCK),
         preferred_element_type=jnp.float32,
     )
-    for h in range(2):
-        for q in range(8):
-            z_out[h * 8 + q] = partial[h * 8 : (h + 1) * 8, q * 128 : (q + 1) * 128]
-    for k in ALONG_Z:
-        other = lax.rem(z + k, NZ)
-        send(z_out.at[other], z_in.at[z], z_send.at[other], z_recv.at[z], at_z(other)).start()
-    for offsets in BULK[CUTS[0] : CUTS[1]]:
-        bulk(offsets).start()
-    z_in[z] = z_out[z]
-
-    for k in ALONG_Z:
-        other = lax.rem(z + k, NZ)
-        send(z_out.at[other], z_in.at[other], z_send.at[other], z_recv.at[other], at_z(other)).wait_recv()
-    total = jnp.sum(z_in[...], axis=0)
-    y_out[...] = total
-    half = lax.rem(z, 8) // 4
-    for k in ALONG_Y:
-        other = lax.rem(y + k, NY)
-
-        @pl.when(other // 4 == half)
-        def _():
-            send(y_out, y_in.at[y], y_send.at[other], y_recv.at[y], at_y(other)).start()
-
-    for offsets in BULK[CUTS[1] : CUTS[2]]:
-        bulk(offsets).start()
-    y_in[y] = total
-
-    @pl.when(y_hi == half)
+    for p in range(16):
+        h, q = p // 8, p % 8
+        z_out[p // 4, p % 4] = partial[h * 8 : (h + 1) * 8, q * 128 : (q + 1) * 128]
+
+    adds = z < ROLES
+    wait_now = adds | corner
+
+    @pl.when(wait_now & (rank < NZ - 1))
+    def _():
+        pl.semaphore_wait(later, NZ - 1 - rank)
+
+    def along(to):
+        return send(z_out.at[to], z_in.at[z], z_send.at[to], z_recv.at[z], at_z(to))
+
+    for to_z in range(ROLES):
+
+        @pl.when(z != to_z)
+        def _():
+            along(to_z).start()
+
+    for i in range(len(EXTRA)):
+        extra(i, False)
+    start(BULK[EXTRA[-1][1] : CUTS[1]])
+    @pl.when((y != 0) & (y != 4))
+    def _():
+        pl.semaphore_wait(line, 1)
+
+    half = lax.rem(z, 2)
+
+    def upright(other):
+        return send(y_out, y_in.at[y], y_send.at[other], y_recv.at[y], at_y(other))
+
+    @pl.when(adds)
+    def _():
+        z_in[z] = z_out[lax.rem(z, ROLES)]
+        for k in ALONG_Z:
+            other = lax.rem(z + k, NZ)
+            send(z_out.at[0], z_in.at[other], z_send.at[0], z_recv.at[other], at_z(other)).wait_recv()
+        total = jnp.sum(z_in[...], axis=0)
+        y_out[...] = total
+        for k in ALONG_Y:
+            other = lax.rem(y + k, NY)
+
+            @pl.when(other // 4 == half)
+            def _():
+                upright(other).start()
+
+        y_in[y] = total
+
+    start(BULK[CUTS[1] : CUTS[2]])
+
+    gives = adds & (y_hi == half)
+
+    def back(other):
+        return send(f_out, f_in.at[z // 2], f_send.at[other], f_recv.at[z // 2], at_z(other))
+
+    @pl.when(gives)
     def _():
         for k in ALONG_Y:
             other = lax.rem(y + k, NY)
@@ -216,46 +331,45 @@
         summed = jnp.sum(y_in[...], axis=0)
         f_out[...] = summed
         for k in ALONG_Z:
-            other = lax.rem(z + k, NZ)
-            send(f_out, f_in.at[z], f_send.at[other], f_recv.at[z], at_z(other)).start()
-        f_in[z] = summed
-
-    for offsets in BULK[CUTS[2] :]:
-        bulk(offsets).start()
+            back(lax.rem(z + k, NZ)).start()
+        f_in[z // 2] = summed
+
+    start(BULK[CUTS[2] :])
 
     for h in range(2):
-        for q in range(4):
-            other = h * 8 + y_hi * 4 + q
-
-            @pl.when(other != z)
-            def _():
-                send(f_out, f_in.at[other], f_send.at[other], f_recv.at[other], at_z(other)).wait_recv()
-
-    for h in range(2):
-        for q in range(4):
-            grad[h * 8 : (h + 1) * 8, q * 128 : (q + 1) * 128] = f_in[h * 8 + y_hi * 4 + q]
+        giver = 2 * h + y_hi
+
+        @pl.when(giver != z)
+        def _():
+            send(f_out, f_in.at[h], f_send.at[0], f_recv.at[h], at_z(giver)).wait_recv()
+
+    for p in range(8):
+        h, q = p // 4, p % 4
+        grad[h * 8 : (h + 1) * 8, q * 128 : (q + 1) * 128] = f_in[h, q]
+
+    @pl.when(jnp.logical_not(wait_now) & (rank < NZ - 1))
+    def _():
+        pl.semaphore_wait(later, NZ - 1 - rank)
 
     for _, dx, dc in NEAR:
-        other = lax.rem(x + dx, NX) * NC + lax.rem(c + dc, NC)
-        send(
-            rows_out.at[other], rows_in.at[row], r_send.at[other], r_recv.at[row],
-            (dp, y_hi * ROW + other),
-        ).wait_send()
-    for k in ALONG_Z:
-        other = lax.rem(z + k, NZ)
-        send(z_out.at[other], z_in.at[z], z_send.at[other], z_recv.at[z], at_z(other)).wait_send()
+        across(lax.rem(x + dx, NX) * NC + lax.rem(c + dc, NC)).wait_send()
+    for to_z in range(ROLES):
+
+        @pl.when(z != to_z)
+        def _():
+            along(to_z).wait_send()
+
     for k in ALONG_Y:
         other = lax.rem(y + k, NY)
 
-        @pl.when(other // 4 == half)
-        def _():
-            send(y_out, y_in.at[y], y_send.at[other], y_recv.at[y], at_y(other)).wait_send()
-
-    @pl.when(y_hi == half)
+        @pl.when(adds & (other // 4 == half))
+        def _():
+            upright(other).wait_send()
+
+    @pl.when(gives)
     def _():
         for k in ALONG_Z:
-            other = lax.rem(z + k, NZ)
-            send(f_out, f_in.at[z], f_send.at[other], f_recv.at[z], at_z(other)).wait_send()
+            back(lax.rem(z + k, NZ)).wait_send()
 
     own.wait()
     for offsets in BULK:
@@ -286,21 +400,21 @@
             pltpu.VMEM((EXPERTS, CAP, D), bf16),
             pltpu.VMEM((ROW, 16, 2 * BLOCK + 128), bf16),
             pltpu.VMEM((ROW, 16, 2 * BLOCK + 128), bf16),
-            pltpu.VMEM((NZ, 8, 128), f32),
-            pltpu.VMEM((NZ, 8, 128), f32),
-            pltpu.VMEM((8, 128), f32),
-            pltpu.VMEM((NY, 8, 128), f32),
-            pltpu.VMEM((8, 128), f32),
-            pltpu.VMEM((NZ, 8, 128), f32),
-            dma((6,)), dma,
-            dma((EXPERTS,)), dma((EXPERTS,)),
+            pltpu.VMEM((ROLES, 4, 8, 128), f32),
+            pltpu.VMEM((NZ, 4, 8, 128), f32),
+            pltpu.VMEM((4, 8, 128), f32),
+            pltpu.VMEM((NY, 4, 8, 128), f32),
+            pltpu.VMEM((4, 8, 128), f32),
+            pltpu.VMEM((2, 4, 8, 128), f32),
+            dma((6,)), dma, pltpu.SemaphoreType.REGULAR, pltpu.SemaphoreType.REGULAR, pltpu.SemaphoreType.REGULAR,
+            dma((EXPERTS, PARTS)), dma((EXPERTS, PARTS)),
             dma((ROW,)), dma((ROW,)),
-            dma((NZ,)), dma((NZ,)),
+            dma((ROLES,)), dma((NZ,)),
             dma((NY,)), dma((NY,)),
-            dma((NZ,)), dma((NZ,)),
+            dma((NZ,)), dma((2,)),
         ],
         compiler_params=pltpu.CompilerParams(
-            collective_id=0, has_side_effects=True, vmem_limit_bytes=24 << 20
+            collective_id=0, has_side_effects=True, vmem_limit_bytes=60 << 20
         ),
         cost_estimate=pl.CostEstimate(
             flops=300_000_000, bytes_accessed=8_000_000, transcendentals=256

time: 92.4 us -> 73 us (0.79)
  the two profiles are of different devices: /device:TPU:52 before, /device:TPU:56 now
where the time goes in v2:
time: 73 us; the launch traced here: 72.8 us
  Pallas kernels  68.4 us (94%)
  local copies, waits for them, and re-layouts  3.75 us (5%)
    pallas_call x1, Pallas kernels, shards(): pl.pallas_call(kernel, out_shape=(jax.ShapeDtypeStruct((EXPERTS, CAP, D),...  68.4 us
    unnamed x4, local copies, waits for them, and re-layouts  3.75 us

profile of v2, /device:TPU:56, one launch (start us, length us, event | category | flops | bytes accessed | tf_op | source)
XLA Modules:
  0.0 72.8 jit_solution(2192384851556701735)
XLA Ops:
  0.6 68.4 %shard_map.77 = (bf16[16,16,4096]{2,1,0:T(8,128)(2,1)}, f32[16,512]{1,0:T(8,128)}) custom-call(bf16[128,4096]{1,0:T(8,128)(2,1)} %d_hbm.1, f32[16,128]{1,0:T(8,128)} %bitcast.7, s32[2,128]{1,0:T(2,128)} %bitcast.8, s32[2,128]{1,0:T(2,128)} %bitcast.9, bf16[16,4096]{1,0:T(8,128)(2,1)} %bitcast.6, bf16[16,8192]{1,0:T(8,128)(2,1)} %channels_hbm.1), custom_call_target="tpu_custom_call" | custom-call | flops 300000000 | bytes 8000000 | tf_op jit(solution)/shard_map/pallas_call | solution.py:385
  69.0 0.0 copy-start
  69.0 3.1 %copy.10 = bf16[1,1,16,16,4096]{4,3,2,1,0:T(8,128)(2,1)} copy(bf16[1,1,16,16,4096]{4,3,2,1,0:T(8,128)(2,1)} %bitcast.5) | data formatting | bytes 4194304
  72.1 0.0 copy-done
  72.1 0.6 copy.11
Async XLA Ops:
  69.0 3.1 %copy-start = (f32[16,512]{1,0:T(8,128)S(1)}, f32[16,512]{1,0:T(8,128)}, u32[]{:S(2)}) copy-start(f32[16,512]{1,0:T(8,128)} %get-tuple-element.9) | copy-start | bytes 98308

commit v3 on v2

--- a/solution.py
+++ b/solution.py
@@ -16,7 +16,7 @@
 NEAR = [(0, dx, dc) for dx in (2, 1, 3, 0) for dc in (0, 1) if (dx, dc) != (0, 0)]
 PEERS = FAR + NEAR
 PARTS = 2
-MIX = [pair[i] for i in range(8) for pair in (FAR, NEAR) if i < len(pair)]
+MIX = (FAR[:3] + NEAR[:1] + FAR[3:5] + NEAR[1:2] + FAR[5:7] + NEAR[2:3] + FAR[7:] + NEAR[3:])
 BULK = [(*offsets, q) for q in range(PARTS) for offsets in MIX]
 FIRST = 1
 EXTRA = ((14, 14, 4),)
@@ -330,8 +330,12 @@
             send(y_out, y_in.at[other], y_send.at[other], y_recv.at[other], at_y(other)).wait_recv()
         summed = jnp.sum(y_in[...], axis=0)
         f_out[...] = summed
-        for k in ALONG_Z:
-            back(lax.rem(z + k, NZ)).start()
+        for to_z in range(NZ):
+
+            @pl.when(z != to_z)
+            def _():
+                back(to_z).start()
+
         f_in[z // 2] = summed
 
     start(BULK[CUTS[2] :])
@@ -385,8 +389,8 @@
     received, grad = pl.pallas_call(
         kernel,
         out_shape=(
-            jax.ShapeDtypeStruct((EXPERTS, CAP, D), bf16),
-            jax.ShapeDtypeStruct((16, BLOCK), f32),
+            pltpu.VMEM((EXPERTS, CAP, D), bf16),
+            pltpu.VMEM((16, BLOCK), f32),
         ),
         in_specs=[in_hbm] * 6,
         out_specs=(anywhere, pl.BlockSpec(memory_space=pltpu.VMEM)),

time: 73 us -> 69.8 us (0.956)
  local copies, waits for them, and re-layouts: 3.75 us -> 1.94 us
  Pallas kernels: 68.4 us -> 67 us
    unnamed x4 -> x2, local copies, waits for them, and re-layouts: 3.75 us -> 1.94 us
    pallas_call x1, Pallas kernels: 68.4 us -> 67 us  [shards(): pl.pallas_call(kernel, out_shape=(pltpu.VMEM((EXPERTS, CAP, D), bf16), pl...]
where the time goes in v3:
time: 69.8 us; the launch traced here: 69.6 us
  Pallas kernels  67 us (96%)
  local copies, waits for them, and re-layouts  1.94 us (3%)
    pallas_call x1, Pallas kernels, shards(): pl.pallas_call(kernel, out_shape=(pltpu.VMEM((EXPERTS, CAP, D), bf16), pl...  67 us
    unnamed x2, local copies, waits for them, and re-layouts  1.94 us

profile of v3, /device:TPU:56, one launch (start us, length us, event | category | flops | bytes accessed | tf_op | source)
XLA Modules:
  0.0 69.6 jit_solution(14087303710283631837)
XLA Ops:
  0.6 67.0 %shard_map.77 = (bf16[16,16,4096]{2,1,0:T(8,128)(2,1)S(1)}, f32[16,512]{1,0:T(8,128)S(1)}) custom-call(bf16[128,4096]{1,0:T(8,128)(2,1)} %d_hbm.1, f32[16,128]{1,0:T(8,128)} %bitcast.7, s32[2,128]{1,0:T(2,128)} %bitcast.8, s32[2,128]{1,0:T(2,128)} %bitcast.9, bf16[16,4096]{1,0:T(8,128)(2,1)} %bitcast.6, bf16[16,8192]{1,0:T(8,128)(2,1)} %channels_hbm.1), custom_call_target="tpu_custom_call" | custom-call | flops 300000000 | bytes 8000000 | tf_op jit(solution)/shard_map/pallas_call | solution.py:389
  67.7 1.3 %copy.10 = bf16[1,1,16,16,4096]{4,3,2,1,0:T(8,128)(2,1)} copy(bf16[1,1,16,16,4096]{4,3,2,1,0:T(8,128)(2,1)S(1)} %bitcast.5) | data formatting | bytes 4194304
  69.0 0.6 copy.11

commit v4 on v3

--- a/solution.py
+++ b/solution.py
@@ -19,11 +19,11 @@
 MIX = (FAR[:3] + NEAR[:1] + FAR[3:5] + NEAR[1:2] + FAR[5:7] + NEAR[2:3] + FAR[7:] + NEAR[3:])
 BULK = [(*offsets, q) for q in range(PARTS) for offsets in MIX]
 FIRST = 1
-EXTRA = ((14, 14, 4),)
-CUTS = (14, 26, 30)
+EXTRA = ((18, 18, 2),)
+CUTS = (18, 30, 30)
 DO_M = True
 ALONG_Z = [s * k % NZ for k in range(1, 9) for s in (1, -1) if not (k == 8 and s < 0)]
-ROLES = 4
+ROLES = 2
 ALONG_Y = (4, 3, 5, 2, 6, 1, 7)
 
 
@@ -269,7 +269,7 @@
     )
     for p in range(16):
         h, q = p // 8, p % 8
-        z_out[p // 4, p % 4] = partial[h * 8 : (h + 1) * 8, q * 128 : (q + 1) * 128]
+        z_out[h, q // 4, q % 4] = partial[h * 8 : (h + 1) * 8, q * 128 : (q + 1) * 128]
 
     adds = z < ROLES
     wait_now = adds | corner
@@ -294,10 +294,8 @@
     def _():
         pl.semaphore_wait(line, 1)
 
-    half = lax.rem(z, 2)
-
     def upright(other):
-        return send(y_out, y_in.at[y], y_send.at[other], y_recv.at[y], at_y(other))
+        return send(y_out.at[other // 4], y_in.at[y], y_send.at[other], y_recv.at[y], at_y(other))
 
     @pl.when(adds)
     def _():
@@ -308,26 +306,21 @@
         total = jnp.sum(z_in[...], axis=0)
         y_out[...] = total
         for k in ALONG_Y:
-            other = lax.rem(y + k, NY)
-
-            @pl.when(other // 4 == half)
-            def _():
-                upright(other).start()
-
-        y_in[y] = total
+            upright(lax.rem(y + k, NY)).start()
+        y_in[y] = jnp.where(y_hi == 0, total[0], total[1])
 
     start(BULK[CUTS[1] : CUTS[2]])
 
-    gives = adds & (y_hi == half)
+    mine = lax.rem(z, ROLES)
 
     def back(other):
-        return send(f_out, f_in.at[z // 2], f_send.at[other], f_recv.at[z // 2], at_z(other))
-
-    @pl.when(gives)
+        return send(f_out, f_in.at[mine], f_send.at[other], f_recv.at[mine], at_z(other))
+
+    @pl.when(adds)
     def _():
         for k in ALONG_Y:
             other = lax.rem(y + k, NY)
-            send(y_out, y_in.at[other], y_send.at[other], y_recv.at[other], at_y(other)).wait_recv()
+            send(y_out.at[0], y_in.at[other], y_send.at[other], y_recv.at[other], at_y(other)).wait_recv()
         summed = jnp.sum(y_in[...], axis=0)
         f_out[...] = summed
         for to_z in range(NZ):
@@ -336,16 +329,15 @@
             def _():
                 back(to_z).start()
 
-        f_in[z // 2] = summed
+        f_in[mine] = summed
 
     start(BULK[CUTS[2] :])
 
     for h in range(2):
-        giver = 2 * h + y_hi
-
-        @pl.when(giver != z)
-        def _():
-            send(f_out, f_in.at[h], f_send.at[0], f_recv.at[h], at_z(giver)).wait_recv()
+
+        @pl.when(z != h)
+        def _():
+            send(f_out, f_in.at[h], f_send.at[0], f_recv.at[h], at_z(h)).wait_recv()
 
     for p in range(8):
         h, q = p // 4, p % 4
@@ -363,15 +355,10 @@
         def _():
             along(to_z).wait_send()
 
-    for k in ALONG_Y:
-        other = lax.rem(y + k, NY)
-
-        @pl.when(adds & (other // 4 == half))
-        def _():
-            upright(other).wait_send()
-
-    @pl.when(gives)
-    def _():
+    @pl.when(adds)
+    def _():
+        for k in ALONG_Y:
+            upright(lax.rem(y + k, NY)).wait_send()
         for k in ALONG_Z:
             back(lax.rem(z + k, NZ)).wait_send()
 
@@ -404,9 +391,9 @@
             pltpu.VMEM((EXPERTS, CAP, D), bf16),
             pltpu.VMEM((ROW, 16, 2 * BLOCK + 128), bf16),
             pltpu.VMEM((ROW, 16, 2 * BLOCK + 128), bf16),
-            pltpu.VMEM((ROLES, 4, 8, 128), f32),
-            pltpu.VMEM((NZ, 4, 8, 128), f32),
-            pltpu.VMEM((4, 8, 128), f32),
+            pltpu.VMEM((ROLES, 2, 4, 8, 128), f32),
+            pltpu.VMEM((NZ, 2, 4, 8, 128), f32),
+            pltpu.VMEM((2, 4, 8, 128), f32),
             pltpu.VMEM((NY, 4, 8, 128), f32),
             pltpu.VMEM((4, 8, 128), f32),
             pltpu.VMEM((2, 4, 8, 128), f32),

time: 69.8 us -> 67.5 us (0.967)
  Pallas kernels: 67 us -> 64.5 us
    pallas_call x1, Pallas kernels: 67 us -> 64.5 us  [shards(): pl.pallas_call(kernel, out_shape=(pltpu.VMEM((EXPERTS, CAP, D), bf16), pl...]
where the time goes in v4:
time: 67.5 us; the launch traced here: 67.1 us
  Pallas kernels  64.5 us (96%)
  local copies, waits for them, and re-layouts  1.94 us (3%)
    pallas_call x1, Pallas kernels, shards(): pl.pallas_call(kernel, out_shape=(pltpu.VMEM((EXPERTS, CAP, D), bf16), pl...  64.5 us
    unnamed x2, local copies, waits for them, and re-layouts  1.94 us

profile of v4, /device:TPU:56, one launch (start us, length us, event | category | flops | bytes accessed | tf_op | source)
XLA Modules:
  0.0 67.1 jit_solution(4688873227209150413)
XLA Ops:
  0.6 64.5 %shard_map.77 = (bf16[16,16,4096]{2,1,0:T(8,128)(2,1)S(1)}, f32[16,512]{1,0:T(8,128)S(1)}) custom-call(bf16[128,4096]{1,0:T(8,128)(2,1)} %d_hbm.1, f32[16,128]{1,0:T(8,128)} %bitcast.7, s32[2,128]{1,0:T(2,128)} %bitcast.8, s32[2,128]{1,0:T(2,128)} %bitcast.9, bf16[16,4096]{1,0:T(8,128)(2,1)} %bitcast.6, bf16[16,8192]{1,0:T(8,128)(2,1)} %channels_hbm.1), custom_call_target="tpu_custom_call" | custom-call | flops 300000000 | bytes 8000000 | tf_op jit(solution)/shard_map/pallas_call | solution.py:376
  65.2 1.3 %copy.10 = bf16[1,1,16,16,4096]{4,3,2,1,0:T(8,128)(2,1)} copy(bf16[1,1,16,16,4096]{4,3,2,1,0:T(8,128)(2,1)S(1)} %bitcast.5) | data formatting | bytes 4194304
  66.5 0.6 copy.11
